TPU v7x, 256 devices: a whole 4x4x8 slice. The times are simulated.
256 devices in a mesh: group: 4 (over y), owner: 64 (over z, x, core).
Axes of the slice: x: 4, y: 4, z: 8, core: 2. Of those that a mesh axis runs over, the one named last changes fastest.
Arguments:
- field: float32 [64, 32768], P(None, ('group', 'owner')), may hold values from -6 to 6
- contrast: float32 [64, 32768], P(None, ('group', 'owner')), may hold values from 0.1 to 2
- incident: float32 [64, 32768], P(None, ('group', 'owner')), may hold values from -6 to 6
- near_lists: int32 [27, 32768], P(None, ('group', 'owner')), may hold values from -1 to 128, as said below
- far_lists: int32 [316, 37376], P(None, ('group', 'owner')), may hold values from -1 to 511, as said below
- near_mats: float32 [27, 64, 64], replicated, may hold values from -0.15625 to 0.15625
- far_mats: float32 [316, 49, 49], replicated, may hold values from -0.0625 to 0.0625
- up_mats: float32 [8, 49, 49], replicated, may hold values from -0.3125 to 0.3125
- down_mats: float32 [8, 49, 49], replicated, may hold values from -0.875 to 0.875
- moment_map: float32 [49, 64], replicated, may hold values from -0.75 to 0.75
- local_map: float32 [64, 49], replicated, may hold values from -0.5 to 0.5
Outputs:
- new_field: float32 [64, 32768], P(None, ('group', 'owner'))
Inputs may be any that keep to these rules, and one draw needn't show every extreme that they name: -1 marks an empty slot; otherwise b + near_lists[k, b] - 64 is a leaf box, and slot 13 of every box holds 64. `far_lists`: -1 marks an empty slot; otherwise the entry names a box of the column's level as the steps say: below level 2 an entry of 0 to w_l, at level 2 any box of that level.
All inputs are finite; a program needn't handle non-finite values.
Results may differ from a plain program's by a relative error of at most 0.0003.
Values sent between devices are 32-bit elements; how exact they have to be, the bound alone decides.
A program may use at most 128 MiB of HBM per device.

v0:
```python
import functools

import jax
import jax.numpy as jnp
from jax import lax
from jax.experimental import pallas as pl
from jax.experimental.pallas import tpu as pltpu
from jax.sharding import PartitionSpec as P

f32, bf16, i32 = jnp.float32, jnp.bfloat16, jnp.int32
MESH = pl.DeviceIdType.MESH
HIGHEST = lax.Precision.HIGHEST

LEAVES = 128
TERMS = 49
SLOTS = 316
WIDE = 384
GROUP = 7
NGROUP = TERMS // GROUP
ROWS = 144
BLOCK = 8


def split(x):
    hi = x.astype(bf16)
    return hi, (x - hi.astype(f32)).astype(bf16)


def take(source, index):
    return jnp.take_along_axis(source, index, axis=1, mode="promise_in_bounds")


def nt(a, b):
    return lax.dot_general(a, b, (((1,), (1,)), ((), ())), precision=HIGHEST, preferred_element_type=f32)


def rows_of_children(ref, count):
    return jnp.concatenate([ref[pl.ds(c, count, stride=8), :] for c in range(8)], axis=1)


def pad_mats(x):
    r, c = x.shape
    x = jnp.concatenate([x, jnp.zeros((r, WIDE - c), x.dtype)], 1)
    return jnp.concatenate([x, jnp.zeros((64 - r, WIDE), x.dtype)], 0)


def prepare_lists(lists, index, code, index2, code2):
    index[:, 256:WIDE] = jnp.zeros((ROWS, 128), i32)
    code[:, 256:WIDE] = jnp.full((ROWS, 128), 2, i32)
    index2[:, :, 256:WIDE] = jnp.zeros((2, 8, 128), i32)
    code2[:, :, 256:WIDE] = jnp.full((2, 8, 128), 4, i32)
    for lo, hi in ((0, 128), (128, 256), (256, SLOTS)):
        e = lists[0:ROWS, lo:hi]
        row = lax.broadcasted_iota(i32, e.shape, 0)
        i = jnp.where(row < LEAVES, row, row - LEAVES) + e
        valid = e >= 0
        index[:, lo:hi] = jnp.where(valid, i & 127, 0)
        code[:, lo:hi] = jnp.where(valid, jnp.where((e == LEAVES), 1, 0), 2)
        for j in range(2):
            e = jnp.broadcast_to(lists[ROWS + j : ROWS + j + 1, lo:hi], (8, hi - lo))
            index2[j, :, lo:hi] = jnp.where(e >= 0, (e >> 1) & 127, 0)
            code2[j, :, lo:hi] = jnp.where(e >= 0, (e & 1) * 2 + (e >> 8), 4)


def prepare_mats(mats, weights, g):
    for ti in range(GROUP):
        x = mats[g * GROUP + ti]
        hi = x.astype(bf16).astype(f32)
        cols = slice(ti * WIDE, (ti + 1) * WIDE)
        weights[g, 0:64, cols] = pad_mats(x).astype(bf16)
        weights[g, 64:128, cols] = pad_mats(x - hi).astype(bf16)


def pick_group(e0b, e1b, xs, index, code, picked, g):
    lane = lax.broadcasted_iota(i32, (16, 128), 1)
    sub = lax.broadcasted_iota(i32, (16, 128), 0)
    for bt in range(9):
        rows = slice(bt * 16, bt * 16 + 16)
        sources = []
        for ti in range(GROUP):
            t = g * GROUP + ti
            if bt < 8:
                own = e0b[t, :, 0:128]
                far = e0b[t, :, 128:256]
                both = [jnp.where(lane[0:8] >= sub[0:8] + (bt * 16 + h * 8), own, far) for h in range(2)]
            else:
                both = [e1b[t], e1b[t]]
            sources.append(jnp.concatenate(both, 0))
        for kt in range(3):
            i = index[rows, kt * 128 : kt * 128 + 128]
            k = code[rows, kt * 128 : kt * 128 + 128]
            for ti in range(GROUP):
                x = take(sources[ti], i)
                if bt < 8:
                    last = xs[rows, ti * 128 : ti * 128 + 128]
                    x = jnp.where(k == 0, x, jnp.where(k == 1, last, 0.0))
                else:
                    x = jnp.where(k == 0, x, 0.0)
                hi, lo = split(x)
                cols = slice(ti * WIDE + kt * 128, ti * WIDE + kt * 128 + 128)
                picked[bt * 16 : bt * 16 + 16, cols] = hi
                picked[ROWS + bt * 16 : ROWS + bt * 16 + 16, cols] = lo


def spread_group(ends, xs, g):
    row = lax.broadcasted_iota(i32, (256, GROUP * 128), 0) & 127
    col = lax.broadcasted_iota(i32, (256, GROUP * 128), 1) >> 7
    select = jnp.where(row == col + g * GROUP, 1.0, 0.0).astype(bf16)
    xs[...] = jnp.dot(ends, select, preferred_element_type=f32)


def dot_group(picked, weights, g):
    return lax.dot_general(picked[...], weights[g], (((1,), (1,)), ((), ())), preferred_element_type=f32)


def kernel(
    shape,
    field, contrast, incident, near_lists, lists, near_mats, far_mats, up, down, moment_map, local_t,
    out,
    mats, weights, picked_a, picked_b, xs_a, xs_b, index, code, index2, code2, total,
    rolled, from_left, from_right, up_cat, down_cat, m0_own, m0_ext, m1_own, m2_own, mine, tops,
    e0, e0b, e1b, near_all, p2, x2, x1,
    mat_sem, halo_send, halo_recv, send1, recv1, send2, recv2, own_sem,
):
    n_group, n_owner = shape
    n = n_group * n_owner
    blocks = n // BLOCK
    rank = lax.axis_index("group") * n_owner + lax.axis_index("owner")

    def at(r):
        return (r // n_owner, r % n_owner)

    left, right = (rank + n - 1) % n, (rank + 1) % n
    base = rank // BLOCK * BLOCK
    slot = rank % BLOCK

    if n < 256:
        tops[...] = jnp.zeros_like(tops)

    def start_mats(t, _):
        pltpu.make_async_copy(far_mats.at[:, t, :], mats.at[t], mat_sem.at[t]).start()
        return 0

    lax.fori_loop(0, TERMS, start_mats, 0)

    def peer1(d):
        return base + (slot + d) % BLOCK

    def peer2(d):
        return (rank + d * BLOCK) % n

    barrier = pltpu.get_barrier_semaphore()
    pl.semaphore_signal(barrier, inc=1, device_id=at(left), device_id_type=MESH)
    pl.semaphore_signal(barrier, inc=1, device_id=at(right), device_id_type=MESH)

    def greet1(d, _):
        pl.semaphore_signal(barrier, inc=1, device_id=at(peer1(d)), device_id_type=MESH)
        return 0

    def greet2(d, _):
        pl.semaphore_signal(barrier, inc=1, device_id=at(peer2(d)), device_id_type=MESH)
        return 0

    lax.fori_loop(1, BLOCK, greet1, 0)
    lax.fori_loop(1, blocks, greet2, 0)

    source = contrast[...] * field[...]
    own_rolled = pltpu.roll(source, 64, 1)
    rolled[...] = own_rolled
    up_cat[...] = jnp.zeros_like(up_cat)
    down_cat[...] = jnp.zeros_like(down_cat)
    for c in range(8):
        up_cat[:, c * 128 : c * 128 + TERMS] = up[:, c, :]
        down_cat[:, c * 128 : c * 128 + TERMS] = down[:, c, :]
    m0_own[...] = jnp.zeros_like(m0_own)
    m1_own[...] = jnp.zeros_like(m1_own)
    m2_own[...] = jnp.zeros_like(m2_own)
    x2[...] = jnp.zeros_like(x2)
    x1[...] = jnp.zeros_like(x1)
    e1b[...] = jnp.zeros_like(e1b)
    m0_ext[...] = jnp.zeros_like(m0_ext)
    m0_own[:, 0:TERMS] = nt(source.T, moment_map[...])
    m1_own[:, 0:TERMS] = nt(rows_of_children(m0_own, 16), up_cat[...])
    m2_own[0:2, 0:TERMS] = nt(rows_of_children(m1_own, 2), up_cat[...])
    mine[...] = m2_own[0:1, :] + pltpu.roll(m2_own[1:2, :], 64, 1)

    pl.semaphore_wait(barrier, 2 + (BLOCK - 1) + (blocks - 1))
    own_copy = pltpu.make_async_copy(mine, tops.at[pl.ds(rank, 1), :], own_sem)
    own_copy.start()

    def first(d, sender):
        return pltpu.make_async_remote_copy(
            src_ref=mine, dst_ref=tops.at[pl.ds(sender, 1), :],
            send_sem=send1.at[d], recv_sem=recv1.at[d], device_id=at(peer1(d)), device_id_type=MESH)

    def second(d, owner):
        block = pl.ds(owner // BLOCK * BLOCK, BLOCK)
        return pltpu.make_async_remote_copy(
            src_ref=tops.at[block, :], dst_ref=tops.at[block, :],
            send_sem=send2.at[d], recv_sem=recv2.at[d], device_id=at(peer2(d)), device_id_type=MESH)

    lax.fori_loop(1, BLOCK, lambda d, _: (first(d, rank).start(), 0)[1], 0)
    to_right = pltpu.make_async_remote_copy(
        src_ref=rolled, dst_ref=from_left, send_sem=halo_send.at[0], recv_sem=halo_recv.at[0],
        device_id=at(right), device_id_type=MESH)
    to_left = pltpu.make_async_remote_copy(
        src_ref=rolled, dst_ref=from_right, send_sem=halo_send.at[1], recv_sem=halo_recv.at[1],
        device_id=at(left), device_id_type=MESH)
    to_right.start()
    to_left.start()

    prepare_lists(lists, index, code, index2, code2)
    own_copy.wait()
    lax.fori_loop(
        1, BLOCK, lambda d, _: (first(d, base + (slot + BLOCK - d) % BLOCK).wait_recv(), 0)[1], 0)
    lax.fori_loop(1, blocks, lambda d, _: (second(d, rank).start(), 0)[1], 0)

    def wait_mats(t, _):
        pltpu.make_async_copy(far_mats.at[:, t, :], mats.at[t], mat_sem.at[t]).wait()
        return 0

    lax.fori_loop(0, TERMS, wait_mats, 0)
    lax.fori_loop(0, NGROUP, lambda g, _: (prepare_mats(mats, weights, g), 0)[1], 0)

    to_right.wait()
    to_left.wait()
    lane = lax.broadcasted_iota(i32, (64, 128), 1)
    ext_a = jnp.where(lane < 64, from_left[...], own_rolled)
    ext_b = jnp.where(lane < 64, own_rolled, from_right[...])
    ext = jnp.concatenate([ext_a, ext_b], 1)
    e0[...] = jnp.dot(moment_map[...], ext, precision=HIGHEST, preferred_element_type=f32)
    for t in range(TERMS):
        e0b[t] = jnp.broadcast_to(e0[t : t + 1, :], (8, 256))
    m0_ext[0:128, 0:TERMS] = e0[:, 0:128].T
    m0_ext[128:256, 0:TERMS] = e0[:, 128:256].T
    e1 = nt(up_cat[...], rows_of_children(m0_ext, 32))
    for t in range(TERMS):
        e1b[t, :, 0:32] = jnp.broadcast_to(e1[t : t + 1, :], (8, 32))
    ends = jnp.concatenate(split(m0_ext[128:256, :]), 1)

    s_hi, s_lo = split(ext)
    n_hi, n_lo = split(near_mats[...].reshape(27 * 64, 64))
    near_all[...] = jnp.dot(
        jnp.concatenate([n_hi, n_hi, n_lo], 1), jnp.concatenate([s_hi, s_lo, s_hi], 0), preferred_element_type=f32)
    near = incident[...]
    for k in range(27):
        e = jnp.broadcast_to(near_lists[k : k + 1, :], (64, 128))
        i = e + lane
        valid = e >= 0
        m = jnp.where(valid, i & 127, 0)
        rows = slice(k * 64, k * 64 + 64)
        near = near + jnp.where(
            valid, jnp.where(i < 128, take(near_all[rows, 0:128], m), take(near_all[rows, 128:256], m)), 0.0)
    out[...] = near

    total[...] = jnp.zeros_like(total)
    spread_group(ends, xs_a, 0)
    pick_group(e0b, e1b, xs_a, index, code, picked_a, 0)

    def far_pair(h, _):
        spread_group(ends, xs_b, 2 * h + 1)
        part = dot_group(picked_a, weights, 2 * h)
        pick_group(e0b, e1b, xs_b, index, code, picked_b, 2 * h + 1)
        total[...] += part
        spread_group(ends, xs_a, 2 * h + 2)
        part = dot_group(picked_b, weights, 2 * h + 1)
        pick_group(e0b, e1b, xs_a, index, code, picked_a, 2 * h + 2)
        total[...] += part
        return 0

    lax.fori_loop(0, NGROUP // 2, far_pair, 0)
    total[...] += dot_group(picked_a, weights, NGROUP - 1)
    both = total[0:ROWS, :] + total[ROWS : 2 * ROWS, :]
    terms = both + pltpu.roll(both, 64, 1)

    lax.fori_loop(1, blocks, lambda d, _: (second(d, (rank + n - d * BLOCK) % n).wait_recv(), 0)[1], 0)
    lax.fori_loop(1, BLOCK, lambda d, _: (first(d, rank).wait_send(), 0)[1], 0)
    lax.fori_loop(1, blocks, lambda d, _: (second(d, rank).wait_send(), 0)[1], 0)
    every = tops[...].T
    for j in range(2):
        for kt in range(3):
            cols = slice(kt * 128, kt * 128 + 128)
            i = jnp.concatenate([index2[j, :, cols]] * 7, 0)
            k = jnp.concatenate([code2[j, :, cols]] * 7, 0)
            x = jnp.zeros((56, 128), f32)
            for q in range(4):
                part = every[(q >> 1) * 64 : (q >> 1) * 64 + 56, (q & 1) * 128 : (q & 1) * 128 + 128]
                x = jnp.where(k == q, take(part, i), x)
            p2[j, :, cols] = x

    sums = [jnp.zeros((TERMS, 128), f32)] * 2 + [jnp.zeros((TERMS, SLOTS - 256), f32)] * 2
    for t in range(TERMS):
        a, b, c = mats[t, :, 0:128], mats[t, :, 128:256], mats[t, :, 256:SLOTS]
        for j in range(2):
            sums[j] = sums[j] + (a * p2[j, t : t + 1, 0:128] + b * p2[j, t : t + 1, 128:256])
            sums[2 + j] = sums[2 + j] + c * p2[j, t : t + 1, 256:SLOTS]
    for j in range(2):
        x2[j * 8 : j * 8 + 8, 0:TERMS] = nt(jnp.ones((8, 128), f32), sums[j]) + nt(
            jnp.ones((8, SLOTS - 256), f32), sums[2 + j])

    def children(parents, count):
        sub = lax.broadcasted_iota(i32, (count, 128), 0) & 7
        spread = jnp.concatenate([jnp.where(sub == c, parents, 0.0) for c in range(8)], 1)
        return nt(spread, down_cat[...])

    x1[:, 0:TERMS] = terms[LEAVES:ROWS, 0:TERMS] + children(x2[...], 16)
    parents = jnp.concatenate([jnp.broadcast_to(x1[j : j + 1, :], (8, 128)) for j in range(16)], 0)
    x0 = terms[0:LEAVES, 0:TERMS] + children(parents, 128)
    out[...] += nt(local_t[...].T, x0)


def body(mesh_shape, field, contrast, incident, near_lists, far_lists, near_mats, far_mats, up_mats, down_mats,
         moment_map, local_map):
    vmem = pl.BlockSpec(memory_space=pltpu.VMEM)
    n = mesh_shape[0] * mesh_shape[1]
    dma = pltpu.SemaphoreType.DMA
    call = pl.pallas_call(
        functools.partial(kernel, mesh_shape),
        out_shape=jax.ShapeDtypeStruct((64, LEAVES), f32),
        in_specs=[vmem] * 6 + [pl.BlockSpec(memory_space=pl.ANY)] + [vmem] * 4,
        out_specs=vmem,
        scratch_shapes=[
            pltpu.VMEM((TERMS, TERMS, SLOTS), f32),
            pltpu.VMEM((NGROUP, 128, GROUP * WIDE), bf16),
            pltpu.VMEM((2 * ROWS, GROUP * WIDE), bf16),
            pltpu.VMEM((2 * ROWS, GROUP * WIDE), bf16),
            pltpu.VMEM((LEAVES, GROUP * 128), f32),
            pltpu.VMEM((LEAVES, GROUP * 128), f32),
            pltpu.VMEM((ROWS, WIDE), i32),
            pltpu.VMEM((ROWS, WIDE), i32),
            pltpu.VMEM((2, 8, WIDE), i32),
            pltpu.VMEM((2, 8, WIDE), i32),
            pltpu.VMEM((2 * ROWS, 128), f32),
            pltpu.VMEM((64, 128), f32),
            pltpu.VMEM((64, 128), f32),
            pltpu.VMEM((64, 128), f32),
            pltpu.VMEM((TERMS, 1024), f32),
            pltpu.VMEM((TERMS, 1024), f32),
            pltpu.VMEM((128, 128), f32),
            pltpu.VMEM((256, 128), f32),
            pltpu.VMEM((16, 128), f32),
            pltpu.VMEM((8, 128), f32),
            pltpu.VMEM((1, 128), f32),
            pltpu.VMEM((256, 128), f32),
            pltpu.VMEM((TERMS, 256), f32),
            pltpu.VMEM((TERMS, 8, 256), f32),
            pltpu.VMEM((TERMS, 8, 128), f32),
            pltpu.VMEM((27 * 64, 256), f32),
            pltpu.VMEM((2, 56, WIDE), f32),
            pltpu.VMEM((16, 128), f32),
            pltpu.VMEM((16, 128), f32),
            dma((TERMS,)), dma((2,)), dma((2,)), dma((BLOCK,)), dma((BLOCK,)),
            dma((n // BLOCK + 1,)), dma((n // BLOCK + 1,)), dma,
        ],
        compiler_params=pltpu.CompilerParams(
            collective_id=0, has_side_effects=True, vmem_limit_bytes=48 * 2**20),
    )
    return call(
        field, contrast, incident, near_lists, far_lists.T, near_mats, jnp.transpose(far_mats, (1, 2, 0)),
        jnp.transpose(up_mats, (1, 0, 2)), jnp.transpose(down_mats, (1, 0, 2)), moment_map, local_map.T)


def solution(mesh):
    line = P(None, ("group", "owner"))
    return jax.shard_map(
        functools.partial(body, (mesh.shape["group"], mesh.shape["owner"])), mesh=mesh,
        in_specs=(line,) * 5 + (P(),) * 6, out_specs=line, check_vma=False)
```

profile of v0, /device:TPU:1, one launch (start us, length us, event | category | flops | bytes accessed | tf_op | source)
XLA Modules:
  0.0 44.1 jit_solution(18036753095627434341)
XLA Ops:
  0.0 0.0 copy-start
  0.0 2.2 %copy-done = f32[316,49,49]{0,2,1:T(8,128)S(1)} copy-done((f32[316,49,49]{0,2,1:T(8,128)S(1)}, f32[316,49,49]{0,2,1:T(8,128)}, u32[]{:S(2)}) %copy-start) | copy-done | bytes 3034888
  2.2 0.0 copy-start.1
  2.2 1.2 %copy-done.1 = f32[27,64,64]{2,1,0:T(8,128)S(1)} copy-done((f32[27,64,64]{2,1,0:T(8,128)S(1)}, f32[27,64,64]{2,1,0:T(8,128)}, u32[]{:S(2)}) %copy-start.1) | copy-done | bytes 442392
  3.4 0.0 copy-start.2
  3.4 0.9 %copy-done.2 = s32[316,146]{0,1:T(8,128)S(1)} copy-done((s32[316,146]{0,1:T(8,128)S(1)}, s32[316,146]{0,1:T(8,128)}, u32[]{:S(2)}) %copy-start.2) | copy-done | bytes 184568
  4.3 0.0 copy-start.3
  4.3 0.9 %copy-done.3 = f32[8,49,49]{2,0,1:T(8,128)S(1)} copy-done((f32[8,49,49]{2,0,1:T(8,128)S(1)}, f32[8,49,49]{2,0,1:T(8,128)}, u32[]{:S(2)}) %copy-start.3) | copy-done | bytes 76856
  5.2 0.0 copy-start.4
  5.2 0.9 %copy-done.4 = f32[8,49,49]{2,0,1:T(8,128)S(1)} copy-done((f32[8,49,49]{2,0,1:T(8,128)S(1)}, f32[8,49,49]{2,0,1:T(8,128)}, u32[]{:S(2)}) %copy-start.4) | copy-done | bytes 76856
  6.2 0.0 copy-start.5
  6.2 0.8 %copy-done.5 = f32[64,128]{1,0:T(8,128)S(1)} copy-done((f32[64,128]{1,0:T(8,128)S(1)}, f32[64,128]{1,0:T(8,128)}, u32[]{:S(2)}) %copy-start.5) | copy-done | bytes 32792
  6.9 0.0 copy-start.6
  6.9 0.8 %copy-done.6 = f32[64,128]{1,0:T(8,128)S(1)} copy-done((f32[64,128]{1,0:T(8,128)S(1)}, f32[64,128]{1,0:T(8,128)}, u32[]{:S(2)}) %copy-start.6) | copy-done | bytes 32792
  7.7 0.0 copy-start.7
  7.7 0.8 %copy-done.7 = f32[64,128]{1,0:T(8,128)S(1)} copy-done((f32[64,128]{1,0:T(8,128)S(1)}, f32[64,128]{1,0:T(8,128)}, u32[]{:S(2)}) %copy-start.7) | copy-done | bytes 32792
  8.4 0.0 copy-start.8
  8.4 0.7 %copy-done.8 = f32[49,64]{1,0:T(8,128)S(1)} copy-done((f32[49,64]{1,0:T(8,128)S(1)}, f32[49,64]{1,0:T(8,128)}, u32[]{:S(2)}) %copy-start.8) | copy-done | bytes 12568
  9.2 0.0 copy-start.9
  9.2 0.7 %copy-done.9 = f32[64,49]{0,1:T(8,128)S(1)} copy-done((f32[64,49]{0,1:T(8,128)S(1)}, f32[64,49]{0,1:T(8,128)}, u32[]{:S(2)}) %copy-start.9) | copy-done | bytes 12568
  9.9 0.0 copy-start.10
  9.9 0.7 %copy-done.10 = s32[27,128]{1,0:T(8,128)S(1)} copy-done((s32[27,128]{1,0:T(8,128)S(1)}, s32[27,128]{1,0:T(8,128)}, u32[]{:S(2)}) %copy-start.10) | copy-done | bytes 13848
  10.7 32.8 %shard_map.109 = f32[64,128]{1,0:T(8,128)S(1)} custom-call(f32[64,128]{1,0:T(8,128)S(1)} %copy-done.5, f32[64,128]{1,0:T(8,128)S(1)} %copy-done.6, f32[64,128]{1,0:T(8,128)S(1)} %copy-done.7, s32[27,128]{1,0:T(8,128)S(1)} %copy-done.10, s32[146,316]{1,0:T(8,128)S(1)} %bitcast.6, f32[27,64,64]{2,1,0:T(8,128)S(1)} %copy-done.1, f32[49,49,316]{2,1,0:T(8,128)S(1)} %bitcast.5, ...), custom_call_target="tpu_custom_call" | custom-call | tf_op jit(solution)/shard_map/pallas_call | solution.py:358
  43.5 0.6 %copy.13 = f32[64,128]{1,0:T(8,128)} copy(f32[64,128]{1,0:T(8,128)S(1)} %shard_map.109) | data formatting | bytes 65536
Async XLA Ops:
  0.0 2.2 %copy-start = (f32[316,49,49]{0,2,1:T(8,128)S(1)}, f32[316,49,49]{0,2,1:T(8,128)}, u32[]{:S(2)}) copy-start(f32[316,49,49]{0,2,1:T(8,128)} %param.17) | copy-start | bytes 9104596
  2.2 1.2 %copy-start.1 = (f32[27,64,64]{2,1,0:T(8,128)S(1)}, f32[27,64,64]{2,1,0:T(8,128)}, u32[]{:S(2)}) copy-start(f32[27,64,64]{2,1,0:T(8,128)} %near_mats.1) | copy-start | bytes 1327108
  3.4 0.9 %copy-start.2 = (s32[316,146]{0,1:T(8,128)S(1)}, s32[316,146]{0,1:T(8,128)}, u32[]{:S(2)}) copy-start(s32[316,146]{0,1:T(8,128)} %param.15) | copy-start | bytes 553636
  4.3 0.9 %copy-start.3 = (f32[8,49,49]{2,0,1:T(8,128)S(1)}, f32[8,49,49]{2,0,1:T(8,128)}, u32[]{:S(2)}) copy-start(f32[8,49,49]{2,0,1:T(8,128)} %param.18) | copy-start | bytes 230500
  5.2 0.9 %copy-start.4 = (f32[8,49,49]{2,0,1:T(8,128)S(1)}, f32[8,49,49]{2,0,1:T(8,128)}, u32[]{:S(2)}) copy-start(f32[8,49,49]{2,0,1:T(8,128)} %param.19) | copy-start | bytes 230500
  6.2 0.8 %copy-start.5 = (f32[64,128]{1,0:T(8,128)S(1)}, f32[64,128]{1,0:T(8,128)}, u32[]{:S(2)}) copy-start(f32[64,128]{1,0:T(8,128)} %field.1) | copy-start | bytes 98308
  6.9 0.8 %copy-start.6 = (f32[64,128]{1,0:T(8,128)S(1)}, f32[64,128]{1,0:T(8,128)}, u32[]{:S(2)}) copy-start(f32[64,128]{1,0:T(8,128)} %contrast.1) | copy-start | bytes 98308
  7.7 0.8 %copy-start.7 = (f32[64,128]{1,0:T(8,128)S(1)}, f32[64,128]{1,0:T(8,128)}, u32[]{:S(2)}) copy-start(f32[64,128]{1,0:T(8,128)} %incident.1) | copy-start | bytes 98308
  8.4 0.7 %copy-start.8 = (f32[49,64]{1,0:T(8,128)S(1)}, f32[49,64]{1,0:T(8,128)}, u32[]{:S(2)}) copy-start(f32[49,64]{1,0:T(8,128)} %moment_map.1) | copy-start | bytes 37636
  9.2 0.7 %copy-start.9 = (f32[64,49]{0,1:T(8,128)S(1)}, f32[64,49]{0,1:T(8,128)}, u32[]{:S(2)}) copy-start(f32[64,49]{0,1:T(8,128)} %param.21) | copy-start | bytes 37636
  9.9 0.7 %copy-start.10 = (s32[27,128]{1,0:T(8,128)S(1)}, s32[27,128]{1,0:T(8,128)}, u32[]{:S(2)}) copy-start(s32[27,128]{1,0:T(8,128)} %near_lists.1) | copy-start | bytes 41476
where the time goes:
time: 44.7 us; the launch traced here: 44.1 us
  Pallas kernels  32.8 us (73%)
  local copies, waits for them, and re-layouts  11.3 us (25%)
    pallas_call x1, Pallas kernels, body(): call(field, contrast, incident, near_lists, far_lists.T, near_mats, jnp.t...  32.8 us
    unnamed x23, local copies, waits for them, and re-layouts  11.3 us

commit v1 on v0

--- a/solution.py
+++ b/solution.py
@@ -34,6 +34,14 @@
     return lax.dot_general(a, b, (((1,), (1,)), ((), ())), precision=HIGHEST, preferred_element_type=f32)
 
 
+def nt3(a, b_parts):
+    rows = a.shape[0]
+    both = lax.dot_general(
+        jnp.concatenate(split(a), 0), b_parts, (((1,), (1,)), ((), ())), preferred_element_type=f32)
+    both = both[0:rows] + both[rows : 2 * rows]
+    return both + pltpu.roll(both, 64, 1)
+
+
 def rows_of_children(ref, count):
     return jnp.concatenate([ref[pl.ds(c, count, stride=8), :] for c in range(8)], axis=1)
 
@@ -44,7 +52,7 @@
     return jnp.concatenate([x, jnp.zeros((64 - r, WIDE), x.dtype)], 0)
 
 
-def prepare_lists(lists, index, code, index2, code2):
+def prepare_lists(lists, index, code, index2, code2, blocks):
     index[:, 256:WIDE] = jnp.zeros((ROWS, 128), i32)
     code[:, 256:WIDE] = jnp.full((ROWS, 128), 2, i32)
     index2[:, :, 256:WIDE] = jnp.zeros((2, 8, 128), i32)
@@ -58,8 +66,9 @@
         code[:, lo:hi] = jnp.where(valid, jnp.where((e == LEAVES), 1, 0), 2)
         for j in range(2):
             e = jnp.broadcast_to(lists[ROWS + j : ROWS + j + 1, lo:hi], (8, hi - lo))
-            index2[j, :, lo:hi] = jnp.where(e >= 0, (e >> 1) & 127, 0)
-            code2[j, :, lo:hi] = jnp.where(e >= 0, (e & 1) * 2 + (e >> 8), 4)
+            place = ((e >> 1) & (BLOCK - 1)) * blocks + (e >> 4)
+            index2[j, :, lo:hi] = jnp.where(e >= 0, place & 127, 0)
+            code2[j, :, lo:hi] = jnp.where(e >= 0, (e & 1) * 2 + (place >> 7), 4)
 
 
 def prepare_mats(mats, weights, g):
@@ -115,119 +124,172 @@
 
 def kernel(
     shape,
-    field, contrast, incident, near_lists, lists, near_mats, far_mats, up, down, moment_map, local_t,
+    field_in, contrast_in, incident_in, near_lists_in, lists_in, near_mats_in, far_mats, up_in, down_in, map_in, local_in,
     out,
+    field, contrast, incident, near_lists, lists, near_mats, up, down, moment_map, local_t,
     mats, weights, picked_a, picked_b, xs_a, xs_b, index, code, index2, code2, total,
-    rolled, from_left, from_right, up_cat, down_cat, m0_own, m0_ext, m1_own, m2_own, mine, tops,
+    rolled, halves, up_cat, down_cat, down_parts, m0_own, m0_ext, m1_own, m2_own, mine, tops,
     e0, e0b, e1b, near_all, p2, x2, x1,
-    mat_sem, halo_send, halo_recv, send1, recv1, send2, recv2, own_sem,
+    in_sem, mat_sem, send, recv, send1, recv1, send2, recv2, own_sem,
 ):
-    n_group, n_owner = shape
-    n = n_group * n_owner
+    n_owner = shape[1]
+    n = shape[0] * n_owner
     blocks = n // BLOCK
     rank = lax.axis_index("group") * n_owner + lax.axis_index("owner")
+    slot, block = rank % BLOCK, rank // BLOCK
+    has_left, has_right = rank > 0, rank < n - 1
 
     def at(r):
         return (r // n_owner, r % n_owner)
 
-    left, right = (rank + n - 1) % n, (rank + 1) % n
-    base = rank // BLOCK * BLOCK
-    slot = rank % BLOCK
-
+    def near_peer(d):
+        return block * BLOCK + (slot + d) % BLOCK
+
+    def line_peer(d):
+        return (rank + d * BLOCK) % n
+
+    pairs = (
+        (field_in, field), (contrast_in, contrast), (map_in, moment_map), (up_in, up), (lists_in, lists),
+        (near_mats_in, near_mats), (near_lists_in, near_lists), (incident_in, incident), (down_in, down),
+        (local_in, local_t))
+    loads = [pltpu.make_async_copy(a, b, in_sem.at[i]) for i, (a, b) in enumerate(pairs)]
+    for load in loads[:4]:
+        load.start()
     if n < 256:
         tops[...] = jnp.zeros_like(tops)
+
+    @pl.when(rank == 0)
+    def _():
+        halves[0] = jnp.zeros((64, LEAVES), f32)
+
+    @pl.when(rank == n - 1)
+    def _():
+        halves[1] = jnp.zeros((64, LEAVES), f32)
+
+    barrier = pltpu.get_barrier_semaphore()
+
+    @pl.when(has_left)
+    def _():
+        pl.semaphore_signal(barrier, inc=1, device_id=at(rank - 1), device_id_type=MESH)
+
+    @pl.when(has_right)
+    def _():
+        pl.semaphore_signal(barrier, inc=1, device_id=at(rank + 1), device_id_type=MESH)
+
+    def greet_line(d, _):
+        pl.semaphore_signal(barrier, inc=1, device_id=at(line_peer(d)), device_id_type=MESH)
+        return 0
+
+    def greet_near(d, _):
+        pl.semaphore_signal(barrier, inc=1, device_id=at(near_peer(d)), device_id_type=MESH)
+        return 0
+
+    lax.fori_loop(1, blocks, greet_line, 0)
+    lax.fori_loop(1, BLOCK, greet_near, 0)
 
     def start_mats(t, _):
         pltpu.make_async_copy(far_mats.at[:, t, :], mats.at[t], mat_sem.at[t]).start()
         return 0
 
+    def wait_mats(t, _):
+        pltpu.make_async_copy(far_mats.at[:, t, :], mats.at[t], mat_sem.at[t]).wait()
+        return 0
+
+    for load in loads[4:]:
+        load.start()
     lax.fori_loop(0, TERMS, start_mats, 0)
-
-    def peer1(d):
-        return base + (slot + d) % BLOCK
-
-    def peer2(d):
-        return (rank + d * BLOCK) % n
-
-    barrier = pltpu.get_barrier_semaphore()
-    pl.semaphore_signal(barrier, inc=1, device_id=at(left), device_id_type=MESH)
-    pl.semaphore_signal(barrier, inc=1, device_id=at(right), device_id_type=MESH)
-
-    def greet1(d, _):
-        pl.semaphore_signal(barrier, inc=1, device_id=at(peer1(d)), device_id_type=MESH)
-        return 0
-
-    def greet2(d, _):
-        pl.semaphore_signal(barrier, inc=1, device_id=at(peer2(d)), device_id_type=MESH)
-        return 0
-
-    lax.fori_loop(1, BLOCK, greet1, 0)
-    lax.fori_loop(1, blocks, greet2, 0)
-
+    for ref in (up_cat, down_cat, m0_own, m0_ext, m1_own, m2_own, x2, x1, e1b, total):
+        ref[...] = jnp.zeros_like(ref)
+
+    for load in loads[:4]:
+        load.wait()
     source = contrast[...] * field[...]
-    own_rolled = pltpu.roll(source, 64, 1)
-    rolled[...] = own_rolled
-    up_cat[...] = jnp.zeros_like(up_cat)
-    down_cat[...] = jnp.zeros_like(down_cat)
+    rolled[...] = pltpu.roll(source, 64, 1)
     for c in range(8):
         up_cat[:, c * 128 : c * 128 + TERMS] = up[:, c, :]
-        down_cat[:, c * 128 : c * 128 + TERMS] = down[:, c, :]
-    m0_own[...] = jnp.zeros_like(m0_own)
-    m1_own[...] = jnp.zeros_like(m1_own)
-    m2_own[...] = jnp.zeros_like(m2_own)
-    x2[...] = jnp.zeros_like(x2)
-    x1[...] = jnp.zeros_like(x1)
-    e1b[...] = jnp.zeros_like(e1b)
-    m0_ext[...] = jnp.zeros_like(m0_ext)
     m0_own[:, 0:TERMS] = nt(source.T, moment_map[...])
     m1_own[:, 0:TERMS] = nt(rows_of_children(m0_own, 16), up_cat[...])
     m2_own[0:2, 0:TERMS] = nt(rows_of_children(m1_own, 2), up_cat[...])
     mine[...] = m2_own[0:1, :] + pltpu.roll(m2_own[1:2, :], 64, 1)
-
-    pl.semaphore_wait(barrier, 2 + (BLOCK - 1) + (blocks - 1))
-    own_copy = pltpu.make_async_copy(mine, tops.at[pl.ds(rank, 1), :], own_sem)
+    own_copy = pltpu.make_async_copy(mine, tops.at[pl.ds(slot * blocks + block, 1), :], own_sem)
     own_copy.start()
+
+    def halo(side, target):
+        return pltpu.make_async_remote_copy(
+            src_ref=rolled, dst_ref=halves.at[side], send_sem=send.at[side], recv_sem=recv.at[side],
+            device_id=at(target), device_id_type=MESH)
 
     def first(d, sender):
         return pltpu.make_async_remote_copy(
-            src_ref=mine, dst_ref=tops.at[pl.ds(sender, 1), :],
-            send_sem=send1.at[d], recv_sem=recv1.at[d], device_id=at(peer1(d)), device_id_type=MESH)
+            src_ref=mine, dst_ref=tops.at[pl.ds(slot * blocks + sender // BLOCK, 1), :],
+            send_sem=send1.at[d], recv_sem=recv1.at[d], device_id=at(line_peer(d)), device_id_type=MESH)
 
     def second(d, owner):
-        block = pl.ds(owner // BLOCK * BLOCK, BLOCK)
+        part = tops.at[pl.ds(owner % BLOCK * blocks, blocks), :]
         return pltpu.make_async_remote_copy(
-            src_ref=tops.at[block, :], dst_ref=tops.at[block, :],
-            send_sem=send2.at[d], recv_sem=recv2.at[d], device_id=at(peer2(d)), device_id_type=MESH)
-
-    lax.fori_loop(1, BLOCK, lambda d, _: (first(d, rank).start(), 0)[1], 0)
-    to_right = pltpu.make_async_remote_copy(
-        src_ref=rolled, dst_ref=from_left, send_sem=halo_send.at[0], recv_sem=halo_recv.at[0],
-        device_id=at(right), device_id_type=MESH)
-    to_left = pltpu.make_async_remote_copy(
-        src_ref=rolled, dst_ref=from_right, send_sem=halo_send.at[1], recv_sem=halo_recv.at[1],
-        device_id=at(left), device_id_type=MESH)
-    to_right.start()
-    to_left.start()
-
-    prepare_lists(lists, index, code, index2, code2)
-    own_copy.wait()
-    lax.fori_loop(
-        1, BLOCK, lambda d, _: (first(d, base + (slot + BLOCK - d) % BLOCK).wait_recv(), 0)[1], 0)
-    lax.fori_loop(1, blocks, lambda d, _: (second(d, rank).start(), 0)[1], 0)
-
-    def wait_mats(t, _):
-        pltpu.make_async_copy(far_mats.at[:, t, :], mats.at[t], mat_sem.at[t]).wait()
-        return 0
-
+            src_ref=part, dst_ref=part,
+            send_sem=send2.at[d], recv_sem=recv2.at[d], device_id=at(near_peer(d)), device_id_type=MESH)
+
+    def send_all():
+        others = (BLOCK - 1) + (blocks - 1)
+        inside = jnp.logical_and(has_left, has_right)
+
+        @pl.when(inside)
+        def _():
+            pl.semaphore_wait(barrier, others + 2)
+
+        @pl.when(jnp.logical_not(inside))
+        def _():
+            pl.semaphore_wait(barrier, others + 1)
+
+        @pl.when(has_right)
+        def _():
+            halo(0, rank + 1).start()
+
+        @pl.when(has_left)
+        def _():
+            halo(1, rank - 1).start()
+
+        lax.fori_loop(1, blocks, lambda d, _: (first(d, rank).start(), 0)[1], 0)
+
+    @pl.when(rank >= n // 2)
+    def _():
+        send_all()
+
+    for load in loads[4:]:
+        load.wait()
+    for c in range(8):
+        down_cat[:, c * 128 : c * 128 + TERMS] = down[:, c, :]
+    d_hi = down_cat[...].astype(bf16).astype(f32)
+    rest = jnp.zeros((64 - TERMS, 1024), f32)
+    down_parts[...] = jnp.concatenate([d_hi, rest, down_cat[...] - d_hi, rest], 0).astype(bf16)
+    prepare_lists(lists, index, code, index2, code2, blocks)
     lax.fori_loop(0, TERMS, wait_mats, 0)
     lax.fori_loop(0, NGROUP, lambda g, _: (prepare_mats(mats, weights, g), 0)[1], 0)
 
-    to_right.wait()
-    to_left.wait()
+    @pl.when(rank < n // 2)
+    def _():
+        send_all()
+
+    @pl.when(has_right)
+    def _():
+        halo(0, rank + 1).wait_send()
+
+    @pl.when(has_left)
+    def _():
+        halo(1, rank - 1).wait_send()
+
+    @pl.when(has_left)
+    def _():
+        halo(0, rank).wait_recv()
+
+    @pl.when(has_right)
+    def _():
+        halo(1, rank).wait_recv()
+
     lane = lax.broadcasted_iota(i32, (64, 128), 1)
-    ext_a = jnp.where(lane < 64, from_left[...], own_rolled)
-    ext_b = jnp.where(lane < 64, own_rolled, from_right[...])
-    ext = jnp.concatenate([ext_a, ext_b], 1)
+    ext = jnp.concatenate(
+        [jnp.where(lane < 64, halves[0], rolled[...]), jnp.where(lane < 64, rolled[...], halves[1])], 1)
     e0[...] = jnp.dot(moment_map[...], ext, precision=HIGHEST, preferred_element_type=f32)
     for t in range(TERMS):
         e0b[t] = jnp.broadcast_to(e0[t : t + 1, :], (8, 256))
@@ -253,7 +315,10 @@
             valid, jnp.where(i < 128, take(near_all[rows, 0:128], m), take(near_all[rows, 128:256], m)), 0.0)
     out[...] = near
 
-    total[...] = jnp.zeros_like(total)
+    own_copy.wait()
+    lax.fori_loop(1, blocks, lambda d, _: (first(d, (rank + n - d * BLOCK) % n).wait_recv(), 0)[1], 0)
+    lax.fori_loop(1, BLOCK, lambda d, _: (second(d, rank).start(), 0)[1], 0)
+
     spread_group(ends, xs_a, 0)
     pick_group(e0b, e1b, xs_a, index, code, picked_a, 0)
 
@@ -273,9 +338,10 @@
     both = total[0:ROWS, :] + total[ROWS : 2 * ROWS, :]
     terms = both + pltpu.roll(both, 64, 1)
 
-    lax.fori_loop(1, blocks, lambda d, _: (second(d, (rank + n - d * BLOCK) % n).wait_recv(), 0)[1], 0)
-    lax.fori_loop(1, BLOCK, lambda d, _: (first(d, rank).wait_send(), 0)[1], 0)
-    lax.fori_loop(1, blocks, lambda d, _: (second(d, rank).wait_send(), 0)[1], 0)
+    lax.fori_loop(1, blocks, lambda d, _: (first(d, rank).wait_send(), 0)[1], 0)
+    lax.fori_loop(1, BLOCK, lambda d, _: (second(d, rank).wait_send(), 0)[1], 0)
+    lax.fori_loop(
+        1, BLOCK, lambda d, _: (second(d, block * BLOCK + (slot + BLOCK - d) % BLOCK).wait_recv(), 0)[1], 0)
     every = tops[...].T
     for j in range(2):
         for kt in range(3):
@@ -301,7 +367,7 @@
     def children(parents, count):
         sub = lax.broadcasted_iota(i32, (count, 128), 0) & 7
         spread = jnp.concatenate([jnp.where(sub == c, parents, 0.0) for c in range(8)], 1)
-        return nt(spread, down_cat[...])
+        return nt3(spread, down_parts[...])[:, 0:TERMS]
 
     x1[:, 0:TERMS] = terms[LEAVES:ROWS, 0:TERMS] + children(x2[...], 16)
     parents = jnp.concatenate([jnp.broadcast_to(x1[j : j + 1, :], (8, 128)) for j in range(16)], 0)
@@ -317,9 +383,19 @@
     call = pl.pallas_call(
         functools.partial(kernel, mesh_shape),
         out_shape=jax.ShapeDtypeStruct((64, LEAVES), f32),
-        in_specs=[vmem] * 6 + [pl.BlockSpec(memory_space=pl.ANY)] + [vmem] * 4,
+        in_specs=[pl.BlockSpec(memory_space=pl.ANY)] * 11,
         out_specs=vmem,
         scratch_shapes=[
+            pltpu.VMEM((64, LEAVES), f32),
+            pltpu.VMEM((64, LEAVES), f32),
+            pltpu.VMEM((64, LEAVES), f32),
+            pltpu.VMEM((27, LEAVES), i32),
+            pltpu.VMEM((ROWS + 2, SLOTS), i32),
+            pltpu.VMEM((27, 64, 64), f32),
+            pltpu.VMEM((TERMS, 8, TERMS), f32),
+            pltpu.VMEM((TERMS, 8, TERMS), f32),
+            pltpu.VMEM((TERMS, 64), f32),
+            pltpu.VMEM((TERMS, 64), f32),
             pltpu.VMEM((TERMS, TERMS, SLOTS), f32),
             pltpu.VMEM((NGROUP, 128, GROUP * WIDE), bf16),
             pltpu.VMEM((2 * ROWS, GROUP * WIDE), bf16),
@@ -332,10 +408,10 @@
             pltpu.VMEM((2, 8, WIDE), i32),
             pltpu.VMEM((2 * ROWS, 128), f32),
             pltpu.VMEM((64, 128), f32),
-            pltpu.VMEM((64, 128), f32),
-            pltpu.VMEM((64, 128), f32),
+            pltpu.VMEM((2, 64, 128), f32),
             pltpu.VMEM((TERMS, 1024), f32),
             pltpu.VMEM((TERMS, 1024), f32),
+            pltpu.VMEM((128, 1024), bf16),
             pltpu.VMEM((128, 128), f32),
             pltpu.VMEM((256, 128), f32),
             pltpu.VMEM((16, 128), f32),
@@ -349,11 +425,11 @@
             pltpu.VMEM((2, 56, WIDE), f32),
             pltpu.VMEM((16, 128), f32),
             pltpu.VMEM((16, 128), f32),
-            dma((TERMS,)), dma((2,)), dma((2,)), dma((BLOCK,)), dma((BLOCK,)),
-            dma((n // BLOCK + 1,)), dma((n // BLOCK + 1,)), dma,
+            dma((10,)), dma((TERMS,)), dma((2,)), dma((2,)), dma((n // BLOCK + 1,)), dma((n // BLOCK + 1,)),
+            dma((BLOCK,)), dma((BLOCK,)), dma,
         ],
         compiler_params=pltpu.CompilerParams(
-            collective_id=0, has_side_effects=True, vmem_limit_bytes=48 * 2**20),
+            collective_id=0, has_side_effects=True, vmem_limit_bytes=63 * 2**20),
     )
     return call(
         field, contrast, incident, near_lists, far_lists.T, near_mats, jnp.transpose(far_mats, (1, 2, 0)),

time: 44.7 us -> 29.2 us (0.65)
  local copies, waits for them, and re-layouts: 11.3 us -> 1.38 us
  Pallas kernels: 32.8 us -> 27.6 us
    unnamed x23 -> x1, local copies, waits for them, and re-layouts: 11.3 us -> 1.38 us
    pallas_call x1, Pallas kernels: 32.8 us -> 27.6 us  [body(): call(field, contrast, incident, near_lists, far_lists.T, near_mats, jnp.t...]
where the time goes in v1:
time: 29.2 us; the launch traced here: 29 us
  Pallas kernels  27.6 us (95%)
  local copies, waits for them, and re-layouts  1.38 us (5%)
    pallas_call x1, Pallas kernels, body(): call(field, contrast, incident, near_lists, far_lists.T, near_mats, jnp.t...  27.6 us
    unnamed x1, local copies, waits for them, and re-layouts  1.38 us

profile of v1, /device:TPU:1, one launch (start us, length us, event | category | flops | bytes accessed | tf_op | source)
XLA Modules:
  0.0 29.0 jit_solution(4961337315875541166)
XLA Ops:
  0.0 27.6 %shard_map.109 = f32[64,128]{1,0:T(8,128)} custom-call(f32[64,128]{1,0:T(8,128)} %field_in.1, f32[64,128]{1,0:T(8,128)} %contrast_in.1, f32[64,128]{1,0:T(8,128)} %incident_in.1, s32[27,128]{1,0:T(8,128)} %near_lists_in.1, s32[146,316]{1,0:T(8,128)} %bitcast.6, f32[27,64,64]{2,1,0:T(8,128)} %near_mats_in.1, f32[49,49,316]{2,1,0:T(8,128)} %bitcast.5, ...), custom_call_target="tpu_custom_call" | custom-call | tf_op jit(solution)/shard_map/pallas_call | solution.py:434
  27.7 1.4 %copy.13 = f32[64,128]{1,0:T(8,128)} copy(f32[64,128]{1,0:T(8,128)} %shard_map.109) | data formatting | bytes 65536

commit v2 on v1

--- a/solution.py
+++ b/solution.py
@@ -18,6 +18,7 @@
 GROUP = 7
 NGROUP = TERMS // GROUP
 ROWS = 144
+FIRST_PAIRS = 1
 BLOCK = 8
 
 
@@ -315,10 +316,6 @@
             valid, jnp.where(i < 128, take(near_all[rows, 0:128], m), take(near_all[rows, 128:256], m)), 0.0)
     out[...] = near
 
-    own_copy.wait()
-    lax.fori_loop(1, blocks, lambda d, _: (first(d, (rank + n - d * BLOCK) % n).wait_recv(), 0)[1], 0)
-    lax.fori_loop(1, BLOCK, lambda d, _: (second(d, rank).start(), 0)[1], 0)
-
     spread_group(ends, xs_a, 0)
     pick_group(e0b, e1b, xs_a, index, code, picked_a, 0)
 
@@ -333,7 +330,13 @@
         total[...] += part
         return 0
 
-    lax.fori_loop(0, NGROUP // 2, far_pair, 0)
+    lax.fori_loop(0, FIRST_PAIRS, far_pair, 0)
+
+    own_copy.wait()
+    lax.fori_loop(1, blocks, lambda d, _: (first(d, (rank + n - d * BLOCK) % n).wait_recv(), 0)[1], 0)
+    lax.fori_loop(1, BLOCK, lambda d, _: (second(d, rank).start(), 0)[1], 0)
+
+    lax.fori_loop(FIRST_PAIRS, NGROUP // 2, far_pair, 0)
     total[...] += dot_group(picked_a, weights, NGROUP - 1)
     both = total[0:ROWS, :] + total[ROWS : 2 * ROWS, :]
     terms = both + pltpu.roll(both, 64, 1)

time: 29.2 us -> 29.1 us (level)
  no operation moved by 1% of the time
where the time goes in v2:
time: 29.1 us; the launch traced here: 28.9 us
  Pallas kernels  27.5 us (95%)
  local copies, waits for them, and re-layouts  1.38 us (5%)
    pallas_call x1, Pallas kernels, body(): call(field, contrast, incident, near_lists, far_lists.T, near_mats, jnp.t...  27.5 us
    unnamed x1, local copies, waits for them, and re-layouts  1.38 us

profile of v2, /device:TPU:1, one launch (start us, length us, event | category | flops | bytes accessed | tf_op | source)
XLA Modules:
  0.0 28.9 jit_solution(1408511462896580959)
XLA Ops:
  0.0 27.5 %shard_map.109 = f32[64,128]{1,0:T(8,128)} custom-call(f32[64,128]{1,0:T(8,128)} %field_in.1, f32[64,128]{1,0:T(8,128)} %contrast_in.1, f32[64,128]{1,0:T(8,128)} %incident_in.1, s32[27,128]{1,0:T(8,128)} %near_lists_in.1, s32[146,316]{1,0:T(8,128)} %bitcast.6, f32[27,64,64]{2,1,0:T(8,128)} %near_mats_in.1, f32[49,49,316]{2,1,0:T(8,128)} %bitcast.5, ...), custom_call_target="tpu_custom_call" | custom-call | tf_op jit(solution)/shard_map/pallas_call | solution.py:437
  27.6 1.4 %copy.13 = f32[64,128]{1,0:T(8,128)} copy(f32[64,128]{1,0:T(8,128)} %shard_map.109) | data formatting | bytes 65536
